TPU v7x, 32 devices: a whole 2x2x4 slice. The times are simulated.
32 devices in a mesh: groups: 2 (over y), wide: 4 (over z), narrow: 4 (over x, core).
Axes of the slice: x: 2, y: 2, z: 4, core: 2. Of those that a mesh axis runs over, the one named last changes fastest.
Arguments:
- environment: float32 [10, 4096, 4096], P('groups', 'wide', 'narrow'), parts along dimension 0, may hold values from -6 to 6
- ket_site: float32 [8192, 2, 512], P(('groups', 'narrow'), None, 'wide'), parts along dimension 0, may hold values from -0.0625 to 0.0625
- bra_site: float32 [8192, 2, 4096], P(('groups', 'wide'), None, 'narrow'), parts along dimension 0, may hold values from -0.0625 to 0.0625
- mpo_table: float32 [16, 5, 5, 2, 2], replicated
- field_index: int32 [2], P('groups'), parts along dimension 0, may hold values from 0 to 15
- owners: int32 [4], P('groups'), parts along dimension 0, may hold values from 0 to 3
Outputs:
- new_panels: float32 [4, 5, 4096, 128], P('groups', None, 'narrow', 'wide'), parts along dimension 0
There are 2 independent parts, one for each index of `groups`. A program takes and returns all parts, laid end to end along the dimension named above; an argument that names none is the same for every part. Nothing has to cross between parts.
All inputs are finite; a program needn't handle non-finite values.
Results may differ from a plain program's by a relative error of at most 0.0001.
Values sent between devices are 32-bit elements; how exact they have to be, the bound alone decides.
A program may use at most 128 MiB of HBM per device.

v0:
```python
import jax
import jax.numpy as jnp
from jax import lax
from jax.sharding import PartitionSpec as P

PANELS = 2


precise = lax.Precision.HIGHEST


def spread(block, axis, source):
    block = jnp.where(lax.axis_index(axis) == source, block, jnp.zeros_like(block))
    return lax.psum(block, axis)


def select_mpo(mpo_table, field_index):
    patterns = jnp.arange(mpo_table.shape[0], dtype=jnp.int32)
    picked = (patterns == field_index[0]).astype(jnp.float32)
    return jnp.einsum("k,kwvst->wvst", picked, mpo_table, precision=precise)


def on_device(environment, ket_site, bra_site, mpo_table, field_index, owners):
    local_mpo = select_mpo(mpo_table, field_index)
    results = []
    for number in range(PANELS):
        summed = lax.psum(
            jnp.einsum(
                "wab,btc->watc",
                environment,
                spread(ket_site, "wide", owners[number]),
                precision=precise,
            ),
            "narrow",
        )
        applied = jnp.einsum("wvst,watc->vasc", local_mpo, summed, precision=precise)
        results.append(
            lax.psum_scatter(
                jnp.einsum("asj,vasc->vjc", bra_site, applied, precision=precise),
                "wide",
                scatter_dimension=2,
                tiled=True,
            )
        )
    return jnp.stack(results)


def solution(mesh):
    placed = (
        P("groups", "wide", "narrow"),
        P(("groups", "narrow"), None, "wide"),
        P(("groups", "wide"), None, "narrow"),
        P(),
        P("groups"),
        P("groups"),
    )
    return jax.shard_map(
        on_device,
        mesh=mesh,
        in_specs=placed,
        out_specs=P("groups", None, "narrow", "wide"),
        check_vma=False,
    )
```

profile of v0, /device:TPU:0, one launch (start us, length us, event | category | flops | bytes accessed | tf_op | source)
XLA Modules:
  0.0 495.5 jit_solution(4158894699648118018)
XLA Ops:
  6.5 1.5 copy.11
  8.0 1.3 fusion.43
  10.7 1.6 broadcast_select_fusion.1
  12.2 0.0 all-reduce.7.cloned.1.call-update
  12.3 0.0 all-reduce.5.cloned.1.call-start
  12.3 89.9 %all-reduce.7.cloned.1.call-done = (f32[1024,2,128]{0,2,1:T(8,128)}, f32[1024,2,128]{0,2,1:T(8,128)}) async-done(((f32[1024,2,128]{0,2,1:T(8,128)}, f32[1024,2,128]{0,2,1:T(8,128)}), (f32[1024,2,128]{0,2,1:T(8,128)}, f32[1024,2,128]{0,2,1:T(8,128)})) %all-reduce.7.cloned.1.call-update) | async-done | bytes 2097168 | tf_op jit(solution)/shard_map/psum | solution.py:14
  102.2 22.3 %fusion.20 = f32[5,1024,2,128]{1,3,0,2:T(8,128)} fusion(f32[5,1024,1024]{2,1,0:T(8,128)} %param.6, f32[1024,2,128]{0,2,1:T(8,128)} %get-tuple-element.7), kind=kOutput, calls=%fused_computation.17 | convolution fusion | flops 16106127360 | bytes 27262976 | tf_op jit(solution)/shard_map/wab,btc->watc/dot_general | solution.py:28
  124.5 19.4 %fusion.17 = f32[5,1024,2,128]{1,3,0,2:T(8,128)} fusion(f32[5,1024,1024]{2,1,0:T(8,128)S(1)} %copy-done.2, f32[1024,2,128]{0,2,1:T(8,128)S(1)} %copy-done.3), kind=kOutput, calls=%fused_computation.16 | convolution fusion | flops 16106127360 | bytes 27262976 | tf_op jit(solution)/shard_map/wab,btc->watc/dot_general | solution.py:28
  143.8 0.0 all-reduce.5.cloned.1.call-update
  143.9 0.0 reduce-scatter.5.cloned.1.call-start
  144.6 0.6 fusion.35
  145.2 0.1 copy.22
  145.3 184.8 %all-reduce.5.cloned.1.call-done = (f32[5,1024,2,128]{1,3,0,2:T(8,128)}, f32[5,1024,2,128]{1,3,0,2:T(8,128)}) async-done(((f32[5,1024,2,128]{1,3,0,2:T(8,128)}, f32[5,1024,2,128]{1,3,0,2:T(8,128)}), (f32[5,1024,2,128]{1,3,0,2:T(8,128)}, f32[5,1024,2,128]{1,3,0,2:T(8,128)})) %all-reduce.5.cloned.1.call-update) | async-done | bytes 10485776 | tf_op jit(solution)/shard_map/psum | solution.py:27
  330.1 18.9 %fusion.14 = f32[5,1024,2,128]{1,0,2,3:T(8,128)S(1)} fusion(f32[5,1024,2,128,1]{1,3,0,2,4:T(8,128)} %bitcast.73, f32[1,5,5,2,2]{1,2,4,3,0:T(8,128)S(1)} %copy.22), kind=kOutput, calls=%fused_computation.14 | convolution fusion | flops 157286400 | bytes 10486160 | tf_op jit(solution)/shard_map/wvst,watc->vasc/dot_general | solution.py:36
  349.0 30.7 %fusion.28 = f32[5,1024,128]{1,2,0:T(8,128)} fusion(f32[1024,2,1024]{2,1,0:T(2,128)} %param.8, f32[5,1024,2,128]{1,0,2,3:T(8,128)S(1)} %fusion.14), kind=kOutput, calls=%fused_computation.19 | convolution fusion | flops 16106127360 | bytes 16252928 | tf_op jit(solution)/shard_map/asj,vasc->vjc/dot_general | solution.py:39
  379.7 0.0 reduce-scatter.5.cloned.1.call-update
  379.7 0.0 reduce-scatter.3.cloned.1.call-start
  379.8 8.3 %copy.23 = f32[5,1024,2,128,1]{3,0,2,4,1:T(8,128)} copy(f32[5,1024,2,128,1]{1,3,0,2,4:T(8,128)} %bitcast.74) | data formatting | bytes 10485760 | tf_op jit(solution)/shard_map/psum | solution.py:27
  388.0 11.3 %convolution_bitcast_fusion = f32[5,1024,2,128]{3,0,2,1:T(8,128)S(1)} fusion(f32[5,1024,2,128,1]{3,0,2,4,1:T(8,128)} %copy.23, f32[1,5,5,2,2]{1,2,4,3,0:T(8,128)S(1)} %copy.22), kind=kOutput, calls=%fused_computation.15 | convolution fusion | flops 157286400 | bytes 10486160 | tf_op jit(solution)/shard_map/wvst,watc->vasc/dot_general | solution.py:36
  399.3 23.6 %fusion.23 = f32[5,1024,128]{1,2,0:T(8,128)} fusion(f32[1024,2,1024]{2,1,0:T(2,128)} %param.8, f32[5,1024,2,128]{3,0,2,1:T(8,128)S(1)} %convolution_bitcast_fusion), kind=kOutput, calls=%fused_computation.18 | convolution fusion | flops 16106127360 | bytes 16252928 | tf_op jit(solution)/shard_map/asj,vasc->vjc/dot_general | solution.py:39
  423.0 0.0 reduce-scatter.3.cloned.1.call-update
  423.0 9.2 %reduce-scatter.5.cloned.1.call-done = f32[5,1024,32]{1,2,0:T(8,128)} async-done(((f32[5,1024,128]{1,2,0:T(8,128)}), f32[5,1024,32]{1,2,0:T(8,128)}) %reduce-scatter.5.cloned.1.call-update) | async-done | bytes 655376 | tf_op jit(solution)/shard_map/reduce_scatter | solution.py:38
  432.1 54.1 %reduce-scatter.3.cloned.1.call-done = f32[5,1024,32]{1,2,0:T(8,128)} async-done(((f32[5,1024,128]{1,2,0:T(8,128)}), f32[5,1024,32]{1,2,0:T(8,128)}) %reduce-scatter.3.cloned.1.call-update) | async-done | bytes 655376 | tf_op jit(solution)/shard_map/reduce_scatter | solution.py:38
  486.2 2.5 pad_maximum_fusion
  (9 shorter events, 0.0 us)
Async XLA Ops:
  6.5 138.0 %copy-start = (f32[16,5,5,2,2]{0,4,3,2,1:T(2,128)S(1)}, f32[16,5,5,2,2]{0,4,3,2,1:T(2,128)}, u32[]{:S(2)}) copy-start(f32[16,5,5,2,2]{0,4,3,2,1:T(2,128)} %param.9) | copy-start | bytes 19204
  6.5 95.6 %all-reduce.7.cloned.1.call-start = ((), (), s32[]{:S(2)}) async-start(), calls=%async_computation.5 | async-start | bytes 4194304 | tf_op jit(solution)/shard_map/psum | solution.py:14
  12.3 317.8 %all-reduce.5.cloned.1.call-start = ((), (), s32[]{:S(2)}) async-start(), calls=%async_computation.4 | async-start | bytes 20971520 | tf_op jit(solution)/shard_map/psum | solution.py:27
  102.2 22.3 %copy-start.2 = (f32[5,1024,1024]{2,1,0:T(8,128)S(1)}, f32[5,1024,1024]{2,1,0:T(8,128)}, u32[]{:S(2)}) copy-start(f32[5,1024,1024]{2,1,0:T(8,128)} %param.6) | copy-start | bytes 62914564
  102.2 22.3 %copy-start.3 = (f32[1024,2,128]{0,2,1:T(8,128)S(1)}, f32[1024,2,128]{0,2,1:T(8,128)}, u32[]{:S(2)}) copy-start(f32[1024,2,128]{0,2,1:T(8,128)} %get-tuple-element.8) | copy-start | bytes 3145732
  143.9 288.3 %reduce-scatter.5.cloned.1.call-start = ((), (), s32[]{:S(2)}) async-start(), calls=%async_computation.3 | async-start | bytes 3276800 | tf_op jit(solution)/shard_map/reduce_scatter | solution.py:38
  379.7 106.5 %reduce-scatter.3.cloned.1.call-start = ((), (), s32[]{:S(2)}) async-start(), calls=%async_computation.2 | async-start | bytes 3276800 | tf_op jit(solution)/shard_map/reduce_scatter | solution.py:38
  388.0 100.7 %copy-start.1 = (f32[16,5,5,2,2]{0,4,3,2,1:T(2,128)S(1)}, f32[16,5,5,2,2]{0,4,3,2,1:T(2,128)}, u32[]{:S(2)}) copy-start(f32[16,5,5,2,2]{0,4,3,2,1:T(2,128)} %param.9) | copy-start | bytes 19204
Sparse Core Ops, SparseCore 0:
  12.4 89.7 all-reduce.6
  144.0 186.0 all-reduce.4
  379.8 52.2 reduce-scatter.4
  434.4 51.7 reduce-scatter.2
where the time goes:
time: 500 us; the launch traced here: 495 us
  waiting for transfers between devices  338 us (68%)
  matrix products  127 us (25%)
  between operations  15.3 us (3%)
  local copies, waits for them, and re-layouts  11.2 us (2%)
    psum x1, waiting for transfers between devices, on_device(): lax.psum(jnp.einsum('wab,btc->watc', environment, spread(ket_site, 'wide'...  185 us
    psum x1, waiting for transfers between devices, spread(): return lax.psum(block, axis)  89.9 us
    reduce_scatter x2, waiting for transfers between devices, on_device(): lax.psum_scatter(jnp.einsum('asj,vasc->vjc', bra_site, applied, precision...  63.2 us
    dot_general x2, matrix products, on_device(): jnp.einsum('asj,vasc->vjc', bra_site, applied, precision=precise)  54.4 us
    dot_general x2, matrix products, on_device(): jnp.einsum('wab,btc->watc', environment, spread(ket_site, 'wide', owners[...  41.6 us
    dot_general x2, matrix products, on_device(): jnp.einsum('wvst,watc->vasc', local_mpo, summed, precision=precise)  30.1 us
  transfers between devices with their start and end apart: 4, of which 4 were waited for; matrix products, arithmetic and copies ran while one was open for 9% of the time, Pallas kernels for 0%

commit v1 on v0

--- a/solution.py
+++ b/solution.py
@@ -1,10 +1,16 @@
+import functools
+
 import jax
 import jax.numpy as jnp
 from jax import lax
+from jax.experimental import pallas as pl
+from jax.experimental.pallas import tpu as pltpu
 from jax.sharding import PartitionSpec as P
 
 PANELS = 2
-
+LINE = 4
+PIECES = 8
+TILE = 256
 
 precise = lax.Precision.HIGHEST
 
@@ -20,7 +26,7 @@
     return jnp.einsum("k,kwvst->wvst", picked, mpo_table, precision=precise)
 
 
-def on_device(environment, ket_site, bra_site, mpo_table, field_index, owners):
+def with_collectives(environment, ket_site, bra_site, mpo_table, field_index, owners):
     local_mpo = select_mpo(mpo_table, field_index)
     results = []
     for number in range(PANELS):
@@ -45,6 +51,353 @@
     return jnp.stack(results)
 
 
+def halves(x):
+    high = x.astype(jnp.bfloat16)
+    return high, (x - high.astype(jnp.float32)).astype(jnp.bfloat16)
+
+
+def times(a, b, b_dim):
+    return lax.dot_general(
+        a, b, (((1,), (b_dim,)), ((), ())), preferred_element_type=jnp.float32
+    )
+
+
+def kernel(
+    bond, phys,
+    ket, env, bra, mpo, owners, out,
+    stage, bra_high, bra_low, stream, ket_parts, partial, from_core, applied, from_x, from_sibling, parts, product, from_z,
+    load_sem, hop_send, hop_recv, core_send, core_recv, x_send, x_recv, share_send, share_recv, z_send, z_recv,
+):
+    group, z, n = lax.axis_index("groups"), lax.axis_index("wide"), lax.axis_index("narrow")
+    x, core = n // 2, n % 2
+    sibling, across = x * 2 + 1 - core, (1 - x) * 2 + core
+    rows, depth = ket.shape
+    panel = rows // phys
+    half = panel // 2
+    piece_rows = rows // PIECES
+    piece = panel // LINE
+    chunks = PANELS * bond
+    width = bra_high.shape[2]
+    high_rows = env.shape[1]
+
+    def remote(src, dst, send, recv, at_z, at_n):
+        return pltpu.make_async_remote_copy(
+            src_ref=src, dst_ref=dst, send_sem=send, recv_sem=recv,
+            device_id=(group, at_z, at_n), device_id_type=pl.DeviceIdType.MESH,
+        )
+
+    barrier = pltpu.get_barrier_semaphore()
+    others = [(z, sibling), (z, across)] + [((z + d) % LINE, n) for d in range(1, LINE)]
+    for at_z, at_n in others:
+        pl.semaphore_signal(barrier, inc=1, device_id=(group, at_z, at_n), device_id_type=pl.DeviceIdType.MESH)
+    pl.semaphore_wait(barrier, len(others))
+
+    near = z // 2
+    far = 1 - near
+
+    def hop_copy(way, q):
+        place = stream.at[way, q]
+        return remote(place, place, hop_send.at[way, q], hop_recv.at[way, q], (z + 1 - 2 * way + LINE) % LINE, n)
+
+    def hop(way, q):
+        position = z + way * (LINE - 1 - 2 * z)
+        mine = ket[pl.ds(pl.multiple_of((q % PIECES) * piece_rows, piece_rows), piece_rows), :]
+
+        @pl.when(position == 0)
+        def _():
+            stream[way, q] = mine
+
+        @pl.when(position > 0)
+        def _():
+            hop_copy(way, q).wait_recv()
+            owned = owners[q // PIECES] == z
+            stream[way, q] = jnp.where(owned, mine, stream[way, q])
+
+        @pl.when(position < LINE - 1)
+        def _():
+            hop_copy(way, q).start()
+
+    def hop_done(way, q):
+        position = z + way * (LINE - 1 - 2 * z)
+
+        @pl.when(position < LINE - 1)
+        def _():
+            hop_copy(way, q).wait_send()
+
+    middle = (z == 1) | (z == 2)
+    total = PANELS * PIECES
+
+    def load(block, slot):
+        return pltpu.make_async_copy(block, stage.at[slot], load_sem.at[slot])
+
+    def load_env(w):
+        return load(env.at[w], w % 2)
+
+    load_env(0).start()
+    load_env(1).start()
+
+    @pl.when(jnp.logical_not(middle))
+    def _():
+        @pl.loop(0, total)
+        def _(q):
+            hop(near, q)
+
+    @pl.when(middle)
+    def _():
+        hop(near, 0)
+
+    def both(q):
+        @pl.when(middle & (q + 1 < total))
+        def _():
+            hop(near, q + 1)
+
+        hop(far, q)
+
+    @pl.loop(0, PIECES)
+    def _(q):
+        both(q)
+
+    def take_panel(p):
+        owner_below = owners[p] <= z
+
+        @pl.loop(0, PIECES)
+        def _(i):
+            q = p * PIECES + i
+            high, low = halves(jnp.where(owner_below, stream[0, q], stream[1, q]))
+            at = pl.multiple_of(i * piece_rows, piece_rows)
+            ket_parts[p, pl.ds(at, piece_rows), :] = high
+            ket_parts[p, pl.ds(pl.multiple_of(rows + at, piece_rows), piece_rows), :] = low
+
+    def core_copy(p, w):
+        return remote(
+            partial.at[w, 1 - core], from_core.at[p, w], core_send.at[p, w], core_recv.at[p, w], z, sibling
+        )
+
+    def contract(p, w):
+        load_env(w).wait()
+
+        @pl.loop(0, high_rows // TILE)
+        def _(tile):
+            at = pl.multiple_of(tile * TILE, TILE)
+            high, low = halves(stage[w % 2, pl.ds(at, TILE), :])
+            wide = times(ket_parts[p], high, 1)
+            result = wide[:rows] + wide[rows:] + times(ket_parts[p, :rows, :], low, 1)
+            for t in range(phys):
+                for k in range(2):
+                    first = t * panel + k * half
+                    partial[w, k, t, :, pl.ds(at, TILE)] = result[first:first + half]
+
+        core_copy(p, w).start()
+
+    take_panel(0)
+
+    @pl.loop(0, bond)
+    def _(w):
+        contract(0, w)
+
+        @pl.when(w + 2 < bond)
+        def _():
+            load_env(w + 2).start()
+
+        both(PIECES + w)
+
+    for s in range(phys):
+        load(bra.at[:, s, :], s).start()
+
+    def x_copy(k):
+        return remote(applied.at[k], from_x.at[k], x_send.at[k], x_recv.at[k], z, across)
+
+    def share_copy(k):
+        return remote(applied.at[k], from_sibling.at[k], share_send.at[k], share_recv.at[k], z, sibling)
+
+    def apply_mpo(p, started):
+        @pl.loop(0, bond)
+        def _(w):
+            core_copy(p, w).wait_recv()
+            partial[w, core] = partial[w, core] + from_core[p, w]
+
+        @pl.loop(0, bond)
+        def _(v):
+            @pl.loop(0, half // 8)
+            def _(r):
+                at = pl.ds(pl.multiple_of(r * 8, 8), 8)
+                given = [[partial[w, core, t, at, :] for t in range(phys)] for w in range(bond)]
+                for s in range(phys):
+                    value = None
+                    for w in range(bond):
+                        for t in range(phys):
+                            term = mpo[((w * bond + v) * phys + s) * phys + t] * given[w][t]
+                            value = term if value is None else value + term
+                    applied[p * bond + v, s, at, :] = value
+
+            @pl.when(v < started)
+            def _():
+                x_copy(p * bond + v).start()
+
+        @pl.loop(0, bond)
+        def _(w):
+            core_copy(p, w).wait_send()
+
+    apply_mpo(0, 2)
+
+    @pl.loop(PIECES + bond, total)
+    def _(q):
+        both(q)
+
+    take_panel(1)
+
+    for s in range(phys):
+        load(bra.at[:, s, :], s).wait()
+
+        @pl.loop(0, high_rows // TILE)
+        def _(tile, s=s):
+            at = pl.ds(pl.multiple_of(tile * TILE, TILE), TILE)
+            high, low = halves(stage[s, at, :])
+            bra_high[s, at, :] = high
+            bra_low[s, at, :] = low
+
+    load_env(0).start()
+    load_env(1).start()
+
+    def sum_narrow(k):
+        x_copy(k).wait()
+        applied[k] = applied[k] + from_x[k]
+        share_copy(k).start()
+
+    def z_copy(k, d):
+        at = (z + d) % LINE
+        return remote(
+            product.at[k % 2, pl.ds(pl.multiple_of(at * piece, piece), piece), :],
+            from_z.at[k, d - 1], z_send.at[k, d - 1], z_recv.at[k, d - 1], at, n,
+        )
+
+    def place(source, k, side):
+        for s in range(phys):
+            high, low = halves(source[k, s])
+            at = pl.multiple_of(side * half, half)
+            parts[s, pl.ds(at, half), :] = high
+            parts[s, pl.ds(pl.multiple_of(panel + at, half), half), :] = low
+
+    def multiply(k):
+        place(applied, k, core)
+        share_copy(k).wait_recv()
+        place(from_sibling, k, 1 - core)
+
+        @pl.when(k >= 2)
+        def _():
+            for d in range(1, LINE):
+                z_copy(k - 2, d).wait_send()
+
+        @pl.loop(0, width // TILE)
+        def _(tile):
+            at = pl.ds(pl.multiple_of(tile * TILE, TILE), TILE)
+            result = None
+            for s in range(phys):
+                wide = times(parts[s], bra_high[s, :, at], 0)
+                term = wide[:panel] + wide[panel:] + times(parts[s, :panel, :], bra_low[s, :, at], 0)
+                result = term if result is None else result + term
+            product[k % 2, :, at] = result
+
+        for d in range(1, LINE):
+            z_copy(k, d).start()
+        out[k] = product[k % 2, pl.ds(pl.multiple_of(z * piece, piece), piece), :]
+
+    early = (bond + 1) // 2
+
+    @pl.loop(0, early)
+    def _(k):
+        sum_narrow(k)
+
+        @pl.when(k + 2 < bond)
+        def _():
+            x_copy(k + 2).start()
+
+        multiply(k)
+        for i in range(2):
+            w = 2 * k + i
+
+            @pl.when(w < bond)
+            def _():
+                contract(1, w)
+
+                @pl.when(w + 2 < bond)
+                def _():
+                    load_env(w + 2).start()
+
+    apply_mpo(1, 0)
+
+    @pl.loop(early, chunks)
+    def _(k):
+        sum_narrow(k)
+
+        @pl.when(k + 2 < chunks)
+        def _():
+            x_copy(k + 2).start()
+
+        multiply(k)
+
+    @pl.loop(0, chunks)
+    def _(k):
+        for d in range(1, LINE):
+            z_copy(k, d).wait_recv()
+        out[k] = (out[k] + from_z[k, 0]) + (from_z[k, 1] + from_z[k, 2])
+        share_copy(k).wait_send()
+
+    for k in (chunks - 2, chunks - 1):
+        for d in range(1, LINE):
+            z_copy(k, d).wait_send()
+
+    @pl.loop(0, total)
+    def _(q):
+        hop_done(0, q)
+        hop_done(1, q)
+
+
+def in_kernel(environment, ket_site, bra_site, mpo_table, field_index, owners):
+    bond, rows, depth = environment.shape
+    phys, panel = ket_site.shape[1:]
+    width = bra_site.shape[2]
+    half, piece, chunks = panel // 2, panel // LINE, PANELS * bond
+    mpo = select_mpo(mpo_table, field_index).reshape(-1)
+    ket = ket_site.transpose(1, 2, 0).reshape(phys * panel, depth)
+    dma, f32, bf16 = pltpu.SemaphoreType.DMA, jnp.float32, jnp.bfloat16
+    vmem = pl.BlockSpec(memory_space=pltpu.VMEM)
+    smem = pl.BlockSpec(memory_space=pltpu.SMEM)
+    hbm = pl.BlockSpec(memory_space=pl.ANY)
+    total = PANELS * PIECES
+    result = pl.pallas_call(
+        functools.partial(kernel, bond, phys),
+        out_shape=jax.ShapeDtypeStruct((chunks, piece, width), f32),
+        in_specs=[vmem, hbm, hbm, smem, smem],
+        out_specs=vmem,
+        scratch_shapes=[
+            pltpu.VMEM((2, rows, depth), f32),
+            pltpu.VMEM((phys, rows, width), bf16),
+            pltpu.VMEM((phys, rows, width), bf16),
+            pltpu.VMEM((2, total, phys * panel // PIECES, depth), f32),
+            pltpu.VMEM((PANELS, 2 * phys * panel, depth), bf16),
+            pltpu.VMEM((bond, 2, phys, half, rows), f32),
+            pltpu.VMEM((PANELS, bond, phys, half, rows), f32),
+            pltpu.VMEM((chunks, phys, half, rows), f32),
+            pltpu.VMEM((chunks, phys, half, rows), f32),
+            pltpu.VMEM((chunks, phys, half, rows), f32),
+            pltpu.VMEM((phys, 2 * panel, rows), bf16),
+            pltpu.VMEM((2, panel, width), f32),
+            pltpu.VMEM((chunks, LINE - 1, piece, width), f32),
+            dma((2,)),
+            dma((2, total)), dma((2, total)),
+            dma((PANELS, bond)), dma((PANELS, bond)),
+            dma((chunks,)), dma((chunks,)),
+            dma((chunks,)), dma((chunks,)),
+            dma((chunks, LINE - 1)), dma((chunks, LINE - 1)),
+        ],
+        compiler_params=pltpu.CompilerParams(
+            collective_id=0, has_side_effects=True, vmem_limit_bytes=62 * 2**20
+        ),
+    )(ket, environment, bra_site, mpo, owners)
+    return result.reshape(PANELS, bond, piece, width).swapaxes(2, 3)
+
+
 def solution(mesh):
     placed = (
         P("groups", "wide", "narrow"),
@@ -54,8 +407,9 @@
         P("groups"),
         P("groups"),
     )
+    fits = mesh.shape["wide"] == LINE and mesh.shape["narrow"] == 4
     return jax.shard_map(
-        on_device,
+        in_kernel if fits else with_collectives,
         mesh=mesh,
         in_specs=placed,
         out_specs=P("groups", None, "narrow", "wide"),

time: 500 us -> 197 us (0.39)
  waiting for transfers between devices: 338 us -> 0 us
  Pallas kernels: 0 us -> 189 us
  matrix products: 127 us -> 0.63 us
  between operations: 15.3 us -> 0.67 us
  local copies, waits for them, and re-layouts: 11.2 us -> 5.77 us
    psum x2 -> x0, waiting for transfers between devices: 275 us -> none  [the longest x1 185 us: on_device(): lax.psum(jnp.einsum('wab,btc->watc', environment, spread(ket_site, 'wide'...]
    pallas_call x0 -> x1, Pallas kernels: none -> 189 us  [in_kernel(): pl.pallas_call(functools.partial(kernel, bond, phys), out_shape=jax.Shape...]
    dot_general x6 -> x0, matrix products: 126 us -> none  [the longest x2 54.4 us: on_device(): jnp.einsum('asj,vasc->vjc', bra_site, applied, precision=precise)]
    reduce_scatter x2 -> x0, waiting for transfers between devices: 63.2 us -> none  [on_device(): lax.psum_scatter(jnp.einsum('asj,vasc->vjc', bra_site, applied, precision...]
    psum x1 -> x0, local copies, waits for them, and re-layouts: 8.25 us -> none  [on_device(): lax.psum(jnp.einsum('wab,btc->watc', environment, spread(ket_site, 'wide'...]
  transfers between devices with their start and end apart: 4 -> 0, of which waited for: 4 -> 0; matrix products, arithmetic and copies ran while one was open for 9% -> 0% of each run, Pallas kernels for 0% -> 0%
where the time goes in v1:
time: 197 us; the launch traced here: 196 us
  Pallas kernels  189 us (96%)
  local copies, waits for them, and re-layouts  5.77 us (3%)
    pallas_call x1, Pallas kernels, in_kernel(): pl.pallas_call(functools.partial(kernel, bond, phys), out_shape=jax.Shape...  189 us

profile of v1, /device:TPU:0, one launch (start us, length us, event | category | flops | bytes accessed | tf_op | source)
XLA Modules:
  0.0 196.3 jit_solution(7083313891366670602)
XLA Ops:
  0.0 0.0 copy-start
  0.7 0.2 copy-done
  0.8 0.6 fusion
  1.5 0.2 copy.11
  1.6 0.7 reshape.10.mpo
  2.3 2.2 %copy.8 = f32[2,128,1024]{2,1,0:T(8,128)} copy(f32[2,128,1024]{1,0,2:T(2,128)} %bitcast.15) | data formatting | bytes 2097152 | tf_op jit(solution)/shard_map/transpose | solution.py:362
  4.5 189.2 %shard_map.64 = f32[10,32,1024]{2,1,0:T(8,128)} custom-call(f32[256,1024]{1,0:T(8,128)} %bitcast.14, f32[5,1024,1024]{2,1,0:T(8,128)} %env.1, f32[1024,2,1024]{2,1,0:T(2,128)} %bra.1, f32[100]{0:T(128)} %reshape.10.mpo, s32[2]{0:T(128)} %owners.1), custom_call_target="tpu_custom_call" | custom-call | tf_op jit(solution)/shard_map/pallas_call | solution.py:368
  193.8 2.5 %copy.16 = f32[2,5,1024,32]{2,3,1,0:T(8,128)} copy(f32[2,5,1024,32]{2,3,1,0:T(8,128)} %bitcast.13) | data formatting | bytes 2621440
Async XLA Ops:
  0.0 0.8 copy-start

commit v2 on v1

--- a/solution.py
+++ b/solution.py
@@ -9,8 +9,11 @@
 
 PANELS = 2
 LINE = 4
-PIECES = 8
+SPLIT = 2
+PIECES = 4
 TILE = 256
+AHEAD = 4
+SLOTS = 4
 
 precise = lax.Precision.HIGHEST
 
@@ -71,12 +74,13 @@
     group, z, n = lax.axis_index("groups"), lax.axis_index("wide"), lax.axis_index("narrow")
     x, core = n // 2, n % 2
     sibling, across = x * 2 + 1 - core, (1 - x) * 2 + core
-    rows, depth = ket.shape
+    rows, depth = ket.shape[0] // SPLIT, ket.shape[1]
     panel = rows // phys
+    units = PANELS * SPLIT
     half = panel // 2
     piece_rows = rows // PIECES
     piece = panel // LINE
-    chunks = PANELS * bond
+    chunks = units * bond
     width = bra_high.shape[2]
     high_rows = env.shape[1]
 
@@ -101,7 +105,7 @@
 
     def hop(way, q):
         position = z + way * (LINE - 1 - 2 * z)
-        mine = ket[pl.ds(pl.multiple_of((q % PIECES) * piece_rows, piece_rows), piece_rows), :]
+        mine = ket[pl.ds(pl.multiple_of((q % (SPLIT * PIECES)) * piece_rows, piece_rows), piece_rows), :]
 
         @pl.when(position == 0)
         def _():
@@ -110,7 +114,7 @@
         @pl.when(position > 0)
         def _():
             hop_copy(way, q).wait_recv()
-            owned = owners[q // PIECES] == z
+            owned = owners[q // (SPLIT * PIECES)] == z
             stream[way, q] = jnp.where(owned, mine, stream[way, q])
 
         @pl.when(position < LINE - 1)
@@ -125,7 +129,7 @@
             hop_copy(way, q).wait_send()
 
     middle = (z == 1) | (z == 2)
-    total = PANELS * PIECES
+    total = units * PIECES
 
     def load(block, slot):
         return pltpu.make_async_copy(block, stage.at[slot], load_sem.at[slot])
@@ -158,7 +162,7 @@
         both(q)
 
     def take_panel(p):
-        owner_below = owners[p] <= z
+        owner_below = owners[p // SPLIT] <= z
 
         @pl.loop(0, PIECES)
         def _(i):
@@ -238,13 +242,11 @@
         def _(w):
             core_copy(p, w).wait_send()
 
-    apply_mpo(0, 2)
+    apply_mpo(0, AHEAD)
 
     @pl.loop(PIECES + bond, total)
     def _(q):
         both(q)
-
-    take_panel(1)
 
     for s in range(phys):
         load(bra.at[:, s, :], s).wait()
@@ -267,7 +269,7 @@
     def z_copy(k, d):
         at = (z + d) % LINE
         return remote(
-            product.at[k % 2, pl.ds(pl.multiple_of(at * piece, piece), piece), :],
+            product.at[k % SLOTS, pl.ds(pl.multiple_of(at * piece, piece), piece), :],
             from_z.at[k, d - 1], z_send.at[k, d - 1], z_recv.at[k, d - 1], at, n,
         )
 
@@ -283,10 +285,10 @@
         share_copy(k).wait_recv()
         place(from_sibling, k, 1 - core)
 
-        @pl.when(k >= 2)
+        @pl.when(k >= SLOTS)
         def _():
             for d in range(1, LINE):
-                z_copy(k - 2, d).wait_send()
+                z_copy(k - SLOTS, d).wait_send()
 
         @pl.loop(0, width // TILE)
         def _(tile):
@@ -296,45 +298,59 @@
                 wide = times(parts[s], bra_high[s, :, at], 0)
                 term = wide[:panel] + wide[panel:] + times(parts[s, :panel, :], bra_low[s, :, at], 0)
                 result = term if result is None else result + term
-            product[k % 2, :, at] = result
+            product[k % SLOTS, :, at] = result
 
         for d in range(1, LINE):
             z_copy(k, d).start()
-        out[k] = product[k % 2, pl.ds(pl.multiple_of(z * piece, piece), piece), :]
-
-    early = (bond + 1) // 2
-
-    @pl.loop(0, early)
-    def _(k):
-        sum_narrow(k)
-
-        @pl.when(k + 2 < bond)
-        def _():
-            x_copy(k + 2).start()
-
-        multiply(k)
-        for i in range(2):
-            w = 2 * k + i
-
-            @pl.when(w < bond)
-            def _():
-                contract(1, w)
-
-                @pl.when(w + 2 < bond)
+        out[k] = product[k % SLOTS, pl.ds(pl.multiple_of(z * piece, piece), piece), :]
+
+    sum_narrow(0)
+
+    @pl.loop(0, units)
+    def _(u):
+        more = u + 1 < units
+
+        @pl.loop(0, bond)
+        def _(i):
+            k = u * bond + i
+            last = i == bond - AHEAD
+
+            @pl.when(k + 1 < chunks)
+            def _():
+                sum_narrow(k + 1)
+
+            @pl.when((k + AHEAD < chunks) & jnp.logical_not(last))
+            def _():
+                x_copy(k + AHEAD).start()
+
+            multiply(k)
+
+            @pl.when(more & (i == 0))
+            def _():
+                take_panel(u + 1)
+
+            @pl.loop(3 * i, 3 * i + 3)
+            def _(w):
+                @pl.when(more & (w < bond))
                 def _():
-                    load_env(w + 2).start()
-
-    apply_mpo(1, 0)
-
-    @pl.loop(early, chunks)
-    def _(k):
-        sum_narrow(k)
-
-        @pl.when(k + 2 < chunks)
-        def _():
-            x_copy(k + 2).start()
-
-        multiply(k)
+                    contract(u + 1, w)
+
+                    @pl.when(w + 2 < bond)
+                    def _():
+                        load_env(w + 2).start()
+
+            @pl.when(more & last)
+            def _():
+                apply_mpo(u + 1, 0)
+
+                @pl.when(u + 2 < units)
+                def _():
+                    load_env(0).start()
+                    load_env(1).start()
+
+            @pl.when((k + AHEAD < chunks) & last)
+            def _():
+                x_copy(k + AHEAD).start()
 
     @pl.loop(0, chunks)
     def _(k):
@@ -343,7 +359,7 @@
         out[k] = (out[k] + from_z[k, 0]) + (from_z[k, 1] + from_z[k, 2])
         share_copy(k).wait_send()
 
-    for k in (chunks - 2, chunks - 1):
+    for k in range(chunks - SLOTS, chunks):
         for d in range(1, LINE):
             z_copy(k, d).wait_send()
 
@@ -357,14 +373,17 @@
     bond, rows, depth = environment.shape
     phys, panel = ket_site.shape[1:]
     width = bra_site.shape[2]
-    half, piece, chunks = panel // 2, panel // LINE, PANELS * bond
     mpo = select_mpo(mpo_table, field_index).reshape(-1)
-    ket = ket_site.transpose(1, 2, 0).reshape(phys * panel, depth)
+    small = panel // (LINE * SPLIT)
+    ket = ket_site.reshape(depth, phys, LINE, SPLIT, small).transpose(3, 1, 2, 4, 0)
+    ket = ket.reshape(phys * panel, depth)
+    units, panel = PANELS * SPLIT, panel // SPLIT
+    half, piece, chunks = panel // 2, panel // LINE, units * bond
     dma, f32, bf16 = pltpu.SemaphoreType.DMA, jnp.float32, jnp.bfloat16
     vmem = pl.BlockSpec(memory_space=pltpu.VMEM)
     smem = pl.BlockSpec(memory_space=pltpu.SMEM)
     hbm = pl.BlockSpec(memory_space=pl.ANY)
-    total = PANELS * PIECES
+    total = units * PIECES
     result = pl.pallas_call(
         functools.partial(kernel, bond, phys),
         out_shape=jax.ShapeDtypeStruct((chunks, piece, width), f32),
@@ -375,18 +394,18 @@
             pltpu.VMEM((phys, rows, width), bf16),
             pltpu.VMEM((phys, rows, width), bf16),
             pltpu.VMEM((2, total, phys * panel // PIECES, depth), f32),
-            pltpu.VMEM((PANELS, 2 * phys * panel, depth), bf16),
+            pltpu.VMEM((units, 2 * phys * panel, depth), bf16),
             pltpu.VMEM((bond, 2, phys, half, rows), f32),
-            pltpu.VMEM((PANELS, bond, phys, half, rows), f32),
+            pltpu.VMEM((units, bond, phys, half, rows), f32),
             pltpu.VMEM((chunks, phys, half, rows), f32),
             pltpu.VMEM((chunks, phys, half, rows), f32),
             pltpu.VMEM((chunks, phys, half, rows), f32),
             pltpu.VMEM((phys, 2 * panel, rows), bf16),
-            pltpu.VMEM((2, panel, width), f32),
+            pltpu.VMEM((SLOTS, panel, width), f32),
             pltpu.VMEM((chunks, LINE - 1, piece, width), f32),
             dma((2,)),
             dma((2, total)), dma((2, total)),
-            dma((PANELS, bond)), dma((PANELS, bond)),
+            dma((units, bond)), dma((units, bond)),
             dma((chunks,)), dma((chunks,)),
             dma((chunks,)), dma((chunks,)),
             dma((chunks, LINE - 1)), dma((chunks, LINE - 1)),
@@ -395,7 +414,8 @@
             collective_id=0, has_side_effects=True, vmem_limit_bytes=62 * 2**20
         ),
     )(ket, environment, bra_site, mpo, owners)
-    return result.reshape(PANELS, bond, piece, width).swapaxes(2, 3)
+    result = result.reshape(PANELS, SPLIT, bond, piece, width).transpose(0, 2, 4, 1, 3)
+    return result.reshape(PANELS, bond, width, SPLIT * piece)
 
 
 def solution(mesh):

time: 197 us -> 199 us (1.010)
  Pallas kernels: 189 us -> 192 us
    pallas_call x1, Pallas kernels: 189 us -> 192 us  [in_kernel(): pl.pallas_call(functools.partial(kernel, bond, phys), out_shape=jax.Shape...]
where the time goes in v2:
time: 199 us
  Pallas kernels  192 us (96%)
  local copies, waits for them, and re-layouts  6.03 us (3%)
    pallas_call x1, Pallas kernels, in_kernel(): pl.pallas_call(functools.partial(kernel, bond, phys), out_shape=jax.Shape...  192 us

profile of v2, /device:TPU:0, one launch (start us, length us, event | category | flops | bytes accessed | tf_op | source)
XLA Modules:
  0.0 199.1 jit_solution(17748056865214545081)
XLA Ops:
  0.0 0.0 copy-start
  0.7 0.2 copy-done
  0.8 0.6 fusion
  1.5 0.2 copy.14
  1.6 0.7 reshape.17.mpo
  2.3 1.5 copy.9
  3.8 1.0 copy.10
  4.8 191.8 %shard_map.64 = f32[20,16,1024]{2,1,0:T(8,128)} custom-call(f32[256,1024]{1,0:T(8,128)} %bitcast.17, f32[5,1024,1024]{2,1,0:T(8,128)} %env.1, f32[1024,2,1024]{2,1,0:T(2,128)} %bra.1, f32[100]{0:T(128)} %reshape.17.mpo, s32[2]{0:T(128)} %owners.1), custom_call_target="tpu_custom_call" | custom-call | tf_op jit(solution)/shard_map/pallas_call | solution.py:387
  196.6 2.5 %copy.11 = f32[2,5,1024,2,16]{2,4,3,1,0:T(8,128)} copy(f32[2,5,1024,2,16]{2,4,1,3,0:T(8,128)} %bitcast.16) | data formatting | bytes 2621440 | tf_op jit(solution)/shard_map/transpose | solution.py:417
Async XLA Ops:
  0.0 0.8 copy-start
